TPU v7x, 512 devices: a whole 4x8x8 slice. The times are simulated.
512 devices in a mesh: grp: 16 (over y, x_hi), mem: 32 (over x_lo, z, core).
Axes of the slice: x: 4 (x_hi: 2, x_lo: 2; x = x_hi * 2 + x_lo), y: 8, z: 8, core: 2. Of those that a mesh axis runs over, the one named last changes fastest.
Arguments:
- embeddings: bfloat16 [524288, 768], P(('grp', 'mem')), may hold values from -6 to 6
- cluster_ids: int32 [524288], P(('grp', 'mem')), may hold values from 0 to 62, as said below
- valid_counts: int32 [512], P(('grp', 'mem')), may hold values from 512 to 1024
Outputs:
- best_cosine: float32 [524288], P(('grp', 'mem'))
Inputs may be any that keep to these rules, and one draw needn't show every extreme that they name: `cluster_ids`: the rows form a cycle (row 524287 is followed by row 0); every cluster is one contiguous run of rows on this cycle.
All inputs are finite; a program needn't handle non-finite values.
Results may differ from a plain program's by a relative error of at most 0.0003.
Values may be sent and summed in bfloat16 or wider, within the bound.
A program may use at most 64 MiB of HBM per device.

v0:
```python
import jax
import jax.numpy as jnp
from jax import lax
from jax.sharding import PartitionSpec as P

ROUNDS = 3


EPS = 1e-06


def from_behind(array, axis, by):
    size = lax.axis_size(axis)
    return lax.ppermute(array, axis, [(i, (i + by) % size) for i in range(size)])


def row_scale(block):
    return lax.rsqrt(jnp.sum(jnp.square(block.astype(jnp.float32)), axis=1) + EPS)


def cosines(left, left_scale, right, right_scale):
    dots = lax.dot_general(
        left, right, (((1,), (1,)), ((), ())), preferred_element_type=jnp.float32
    )
    return dots * left_scale[:, None] * right_scale[None, :]


def shards(embeddings, cluster_ids, valid_counts):
    rows = embeddings.shape[0]
    positions = lax.broadcasted_iota(jnp.int32, (rows,), 0)
    own_valid = positions < valid_counts[0]
    own_scale = row_scale(embeddings)
    cosine = cosines(embeddings, own_scale, embeddings, own_scale)
    keep = (
        (cluster_ids[:, None] == cluster_ids[None, :])
        & own_valid[None, :]
        & (positions[:, None] != positions[None, :])
    )
    best = jnp.max(jnp.where(keep, cosine, -2.0), axis=1)
    for offset in range(1, ROUNDS + 1):
        upper_rows, upper_ids, upper_count = from_behind(
            (embeddings, cluster_ids, valid_counts), ("grp", "mem"), -offset
        )
        upper_valid = positions < upper_count[0]
        cosine = cosines(embeddings, own_scale, upper_rows, row_scale(upper_rows))
        same = cluster_ids[:, None] == upper_ids[None, :]
        best = jnp.maximum(
            best, jnp.max(jnp.where(same & upper_valid[None, :], cosine, -2.0), axis=1)
        )
        column_best = jnp.max(jnp.where(same & own_valid[:, None], cosine, -2.0), axis=0)
        arrived = from_behind(column_best, ("grp", "mem"), offset)
        best = jnp.maximum(best, arrived)
    return best


def solution(mesh):
    placed = (P(("grp", "mem"), None), P(("grp", "mem")), P(("grp", "mem")))
    return jax.shard_map(
        shards, mesh=mesh, in_specs=placed, out_specs=P(("grp", "mem")), check_vma=False
    )
```

profile of v0, /device:TPU:1, one launch (start us, length us, event | category | flops | bytes accessed | tf_op | source)
XLA Modules:
  0.0 158.1 jit_solution(14434308928354445548)
XLA Ops:
  0.0 0.0 copy-start
  0.0 17.3 %collective-permute-start.10 = (bf16[1024,768]{1,0:T(8,128)(2,1)}, bf16[1024,768]{1,0:T(8,128)(2,1)S(1)}, u32[]{:S(2)}, u32[]{:S(2)}) collective-permute-start(bf16[1024,768]{1,0:T(8,128)(2,1)} %param.3), channel_id=1, source_target_pairs={{0,509},{1,510},{2,511},{3,0},{4,1},{5,2},{6,3},{7,4},{8,5},{9,6},... | collective-permute-start | bytes 4718600 | tf_op jit(solution)/shard_map/ppermute | solution.py:14
  17.3 1.9 %collective-permute-start.2 = (bf16[1024,768]{1,0:T(8,128)(2,1)}, bf16[1024,768]{1,0:T(8,128)(2,1)S(1)}, u32[]{:S(2)}, u32[]{:S(2)}) collective-permute-start(bf16[1024,768]{1,0:T(8,128)(2,1)} %param.3), channel_id=1, source_target_pairs={{0,511},{1,0},{2,1},{3,2},{4,3},{5,4},{6,5},{7,6},{8,7},{9,8},{10,... | collective-permute-start | bytes 4718600 | tf_op jit(solution)/shard_map/ppermute | solution.py:14
  19.2 2.7 %collective-permute-start.9 = (s32[1]{0:T(128)}, s32[1]{0:T(128)}, u32[]{:S(2)}, u32[]{:S(2)}) collective-permute-start(s32[1]{0:T(128)} %param.5), channel_id=1, source_target_pairs={{0,509},{1,510},{2,511},{3,0},{4,1},{5,2},{6,3},{7,4},{8,5},{9,6},... | collective-permute-start | bytes 20 | tf_op jit(solution)/shard_map/ppermute | solution.py:14
  22.0 1.9 %collective-permute-start.1 = (s32[1]{0:T(128)}, s32[1]{0:T(128)}, u32[]{:S(2)}, u32[]{:S(2)}) collective-permute-start(s32[1]{0:T(128)} %param.5), channel_id=1, source_target_pairs={{0,511},{1,0},{2,1},{3,2},{4,3},{5,4},{6,5},{7,6},{8,7},{9,8},{10,... | collective-permute-start | bytes 20 | tf_op jit(solution)/shard_map/ppermute | solution.py:14
  23.9 2.2 %collective-permute-start.6 = (bf16[1024,768]{1,0:T(8,128)(2,1)}, bf16[1024,768]{1,0:T(8,128)(2,1)S(1)}, u32[]{:S(2)}, u32[]{:S(2)}) collective-permute-start(bf16[1024,768]{1,0:T(8,128)(2,1)} %param.3), channel_id=1, source_target_pairs={{0,510},{1,511},{2,0},{3,1},{4,2},{5,3},{6,4},{7,5},{8,6},{9,7},{1... | collective-permute-start | bytes 4718600 | tf_op jit(solution)/shard_map/ppermute | solution.py:14
  26.7 1.8 %multiply_reduce_fusion.3 = f32[1024]{0:T(1024)S(1)} fusion(bf16[1024,768]{1,0:T(8,128)(2,1)} %param.3), kind=kLoop, calls=%fused_computation.21 | loop fusion | flops 2358272 | bytes 1576960 | tf_op jit(solution)/shard_map/reduce_sum | solution.py:18
  28.5 63.7 %collective-permute-done.9 = s32[1]{0:T(128)} collective-permute-done((s32[1]{0:T(128)}, s32[1]{0:T(128)}, u32[]{:S(2)}, u32[]{:S(2)}) %collective-permute-start.9) | collective-permute-done | bytes 36 | tf_op jit(solution)/shard_map/ppermute | solution.py:14
  92.3 1.9 %collective-permute-start.5 = (s32[1]{0:T(128)}, s32[1]{0:T(128)}, u32[]{:S(2)}, u32[]{:S(2)}) collective-permute-start(s32[1]{0:T(128)} %param.5), channel_id=1, source_target_pairs={{0,510},{1,511},{2,0},{3,1},{4,2},{5,3},{6,4},{7,5},{8,6},{9,7},{1... | collective-permute-start | bytes 20 | tf_op jit(solution)/shard_map/ppermute | solution.py:14
  94.2 0.7 iota_compare_fusion.1
  94.9 0.0 collective-permute-done.1
  94.9 13.1 %collective-permute-start.8 = (s32[1024]{0:T(1024)}, s32[1024]{0:T(1024)S(1)}, u32[]{:S(2)}, u32[]{:S(2)}) collective-permute-start(s32[1024]{0:T(1024)} %param.4), channel_id=1, source_target_pairs={{0,509},{1,510},{2,511},{3,0},{4,1},{5,2},{6,3},{7,4},{8,5},{9,6},... | collective-permute-start | bytes 12296 | tf_op jit(solution)/shard_map/ppermute | solution.py:14
  108.0 0.6 iota_compare_fusion.3
  108.6 0.0 collective-permute-done.5
  108.6 12.9 %collective-permute-start = (s32[1024]{0:T(1024)}, s32[1024]{0:T(1024)S(1)}, u32[]{:S(2)}, u32[]{:S(2)}) collective-permute-start(s32[1024]{0:T(1024)} %param.4), channel_id=1, source_target_pairs={{0,511},{1,0},{2,1},{3,2},{4,3},{5,4},{6,5},{7,6},{8,7},{9,8},{10,... | collective-permute-start | bytes 12296 | tf_op jit(solution)/shard_map/ppermute | solution.py:14
  121.5 0.6 iota_compare_fusion.2
  122.2 0.0 collective-permute-done.10
  122.2 9.7 %collective-permute-start.4 = (s32[1024]{0:T(1024)}, s32[1024]{0:T(1024)S(1)}, u32[]{:S(2)}, u32[]{:S(2)}) collective-permute-start(s32[1024]{0:T(1024)} %param.4), channel_id=1, source_target_pairs={{0,510},{1,511},{2,0},{3,1},{4,2},{5,3},{6,4},{7,5},{8,6},{9,7},{1... | collective-permute-start | bytes 12296 | tf_op jit(solution)/shard_map/ppermute | solution.py:14
  131.9 0.4 multiply_reduce_fusion
  132.3 0.0 collective-permute-done.2
  132.3 0.4 multiply_reduce_fusion.2
  132.7 0.0 copy-done
  132.7 1.8 %fusion.1 = f32[1024,1024]{0,1:T(8,128)S(1)} fusion(bf16[1024,768]{1,0:T(8,128)(2,1)S(1)} %copy-done, bf16[1024,768]{1,0:T(8,128)(2,1)S(1)} %collective-permute-done.2), kind=kOutput, calls=%fused_computation.31 | convolution fusion | flops 1610612736 | bytes 7340032 | tf_op jit(solution)/shard_map/dot_general | solution.py:22
  134.5 0.0 collective-permute-done.6
  134.5 0.4 multiply_reduce_fusion.1
  134.9 0.0 copy-start.1
  134.9 1.8 %fusion.2 = f32[1024,1024]{0,1:T(8,128)S(1)} fusion(bf16[1024,768]{1,0:T(8,128)(2,1)S(1)} %copy-done, bf16[1024,768]{1,0:T(8,128)(2,1)S(1)} %collective-permute-done.6), kind=kOutput, calls=%fused_computation.32 | convolution fusion | flops 1610612736 | bytes 7340032 | tf_op jit(solution)/shard_map/dot_general | solution.py:22
  136.8 0.0 collective-permute-done.8
  136.8 0.0 collective-permute-done
  136.8 0.0 collective-permute-done.4
  136.8 0.0 copy-done.1
  136.8 9.0 %select_reduce_fusion.1 = (f32[1024]{0:T(1024)S(1)}, f32[1024]{0:T(1024)S(1)}, f32[1024]{0:T(1024)S(1)}, f32[1024]{0:T(1024)S(1)}, f32[1024]{0:T(1024)S(1)}, /*index=5*/f32[1024]{0:T(1024)S(1)}) fusion(f32[1024]{0:T(1024)S(1)} %add_rsqrt_fusion, f32[1024]{0:T(1024)S(1)} %add_rsqrt_fusion.3, s32[1024]{0:T(1024)S(1)} %copy-done.1, ...), kind=kOutput, calls=%fused_computation.7 | convolution fusion | flops 1638918144 | bytes 11595776 | tf_op jit(solution)/shard_map/dot_general | solution.py:22
  145.8 1.9 %collective-permute-start.11 = (f32[1024]{0:T(1024)S(1)}, f32[1024]{0:T(1024)S(1)}, u32[]{:S(2)}, u32[]{:S(2)}) collective-permute-start(f32[1024]{0:T(1024)S(1)} %get-tuple-element.10), channel_id=1, source_target_pairs={{0,3},{1,4},{2,5},{3,6},{4,7},{5,8},{6,9},{7,10},{8,11},{9,12},{10... | collective-permute-start | bytes 12296 | tf_op jit(solution)/shard_map/ppermute | solution.py:14
  147.7 1.9 %collective-permute-start.7 = (f32[1024]{0:T(1024)S(1)}, f32[1024]{0:T(1024)S(1)}, u32[]{:S(2)}, u32[]{:S(2)}) collective-permute-start(f32[1024]{0:T(1024)S(1)} %get-tuple-element.13), channel_id=1, source_target_pairs={{0,2},{1,3},{2,4},{3,5},{4,6},{5,7},{6,8},{7,9},{8,10},{9,11},{10,... | collective-permute-start | bytes 12296 | tf_op jit(solution)/shard_map/ppermute | solution.py:14
  149.6 1.9 %collective-permute-start.3 = (f32[1024]{0:T(1024)S(1)}, f32[1024]{0:T(1024)S(1)}, u32[]{:S(2)}, u32[]{:S(2)}) collective-permute-start(f32[1024]{0:T(1024)S(1)} %get-tuple-element.11), channel_id=1, source_target_pairs={{0,1},{1,2},{2,3},{3,4},{4,5},{5,6},{6,7},{7,8},{8,9},{9,10},{10,1... | collective-permute-start | bytes 12296 | tf_op jit(solution)/shard_map/ppermute | solution.py:14
  151.6 3.0 %select_reduce_fusion.6 = f32[1024]{0:T(1024)S(1)} fusion(bf16[1024,768]{1,0:T(8,128)(2,1)S(1)} %copy-done, f32[1024]{0:T(1024)S(1)} %add_rsqrt_fusion.3, s32[1024]{0:T(1024)S(1)} %copy-done.1, pred[1024]{0:T(1024)(128)(4,1)S(1)} %iota_compare_fusion.4), kind=kOutput, calls=%fused_computation.15 | convolution fusion | flops 1619000320 | bytes 1586176 | tf_op jit(solution)/shard_map/dot_general | solution.py:22
  154.5 1.6 %collective-permute-done.11 = f32[1024]{0:T(1024)S(1)} collective-permute-done((f32[1024]{0:T(1024)S(1)}, f32[1024]{0:T(1024)S(1)}, u32[]{:S(2)}, u32[]{:S(2)}) %collective-permute-start.11) | collective-permute-done | bytes 4128 | tf_op jit(solution)/shard_map/ppermute | solution.py:14
  156.1 1.4 collective-permute-done.7
  157.5 0.0 collective-permute-done.3
  157.5 0.6 maximum_maximum_fusion
  (5 shorter events, 0.0 us)
Async XLA Ops:
  0.0 132.7 %copy-start = (bf16[1024,768]{1,0:T(8,128)(2,1)S(1)}, bf16[1024,768]{1,0:T(8,128)(2,1)}, u32[]{:S(2)}) copy-start(bf16[1024,768]{1,0:T(8,128)(2,1)} %param.3) | copy-start | bytes 4718596
  0.0 122.2 %collective-permute-start.10 = (bf16[1024,768]{1,0:T(8,128)(2,1)}, bf16[1024,768]{1,0:T(8,128)(2,1)S(1)}, u32[]{:S(2)}, u32[]{:S(2)}) collective-permute-start(bf16[1024,768]{1,0:T(8,128)(2,1)} %param.3), channel_id=1, source_target_pairs={{0,509},{1,510},{2,511},{3,0},{4,1},{5,2},{6,3},{7,4},{8,5},{9,6},... | collective-permute-start | bytes 4718600 | tf_op jit(solution)/shard_map/ppermute | solution.py:14
  17.3 115.0 %collective-permute-start.2 = (bf16[1024,768]{1,0:T(8,128)(2,1)}, bf16[1024,768]{1,0:T(8,128)(2,1)S(1)}, u32[]{:S(2)}, u32[]{:S(2)}) collective-permute-start(bf16[1024,768]{1,0:T(8,128)(2,1)} %param.3), channel_id=1, source_target_pairs={{0,511},{1,0},{2,1},{3,2},{4,3},{5,4},{6,5},{7,6},{8,7},{9,8},{10,... | collective-permute-start | bytes 4718600 | tf_op jit(solution)/shard_map/ppermute | solution.py:14
  19.2 73.1 %collective-permute-start.9 = (s32[1]{0:T(128)}, s32[1]{0:T(128)}, u32[]{:S(2)}, u32[]{:S(2)}) collective-permute-start(s32[1]{0:T(128)} %param.5), channel_id=1, source_target_pairs={{0,509},{1,510},{2,511},{3,0},{4,1},{5,2},{6,3},{7,4},{8,5},{9,6},... | collective-permute-start | bytes 20 | tf_op jit(solution)/shard_map/ppermute | solution.py:14
  22.0 72.9 %collective-permute-start.1 = (s32[1]{0:T(128)}, s32[1]{0:T(128)}, u32[]{:S(2)}, u32[]{:S(2)}) collective-permute-start(s32[1]{0:T(128)} %param.5), channel_id=1, source_target_pairs={{0,511},{1,0},{2,1},{3,2},{4,3},{5,4},{6,5},{7,6},{8,7},{9,8},{10,... | collective-permute-start | bytes 20 | tf_op jit(solution)/shard_map/ppermute | solution.py:14
  23.9 110.6 %collective-permute-start.6 = (bf16[1024,768]{1,0:T(8,128)(2,1)}, bf16[1024,768]{1,0:T(8,128)(2,1)S(1)}, u32[]{:S(2)}, u32[]{:S(2)}) collective-permute-start(bf16[1024,768]{1,0:T(8,128)(2,1)} %param.3), channel_id=1, source_target_pairs={{0,510},{1,511},{2,0},{3,1},{4,2},{5,3},{6,4},{7,5},{8,6},{9,7},{1... | collective-permute-start | bytes 4718600 | tf_op jit(solution)/shard_map/ppermute | solution.py:14
  92.3 16.3 %collective-permute-start.5 = (s32[1]{0:T(128)}, s32[1]{0:T(128)}, u32[]{:S(2)}, u32[]{:S(2)}) collective-permute-start(s32[1]{0:T(128)} %param.5), channel_id=1, source_target_pairs={{0,510},{1,511},{2,0},{3,1},{4,2},{5,3},{6,4},{7,5},{8,6},{9,7},{1... | collective-permute-start | bytes 20 | tf_op jit(solution)/shard_map/ppermute | solution.py:14
  94.9 41.9 %collective-permute-start.8 = (s32[1024]{0:T(1024)}, s32[1024]{0:T(1024)S(1)}, u32[]{:S(2)}, u32[]{:S(2)}) collective-permute-start(s32[1024]{0:T(1024)} %param.4), channel_id=1, source_target_pairs={{0,509},{1,510},{2,511},{3,0},{4,1},{5,2},{6,3},{7,4},{8,5},{9,6},... | collective-permute-start | bytes 12296 | tf_op jit(solution)/shard_map/ppermute | solution.py:14
  108.6 28.2 %collective-permute-start = (s32[1024]{0:T(1024)}, s32[1024]{0:T(1024)S(1)}, u32[]{:S(2)}, u32[]{:S(2)}) collective-permute-start(s32[1024]{0:T(1024)} %param.4), channel_id=1, source_target_pairs={{0,511},{1,0},{2,1},{3,2},{4,3},{5,4},{6,5},{7,6},{8,7},{9,8},{10,... | collective-permute-start | bytes 12296 | tf_op jit(solution)/shard_map/ppermute | solution.py:14
  122.2 14.6 %collective-permute-start.4 = (s32[1024]{0:T(1024)}, s32[1024]{0:T(1024)S(1)}, u32[]{:S(2)}, u32[]{:S(2)}) collective-permute-start(s32[1024]{0:T(1024)} %param.4), channel_id=1, source_target_pairs={{0,510},{1,511},{2,0},{3,1},{4,2},{5,3},{6,4},{7,5},{8,6},{9,7},{1... | collective-permute-start | bytes 12296 | tf_op jit(solution)/shard_map/ppermute | solution.py:14
  134.9 1.9 %copy-start.1 = (s32[1024]{0:T(1024)S(1)}, s32[1024]{0:T(1024)}, u32[]{:S(2)}) copy-start(s32[1024]{0:T(1024)} %param.4) | copy-start | bytes 12292
  145.8 10.4 %collective-permute-start.11 = (f32[1024]{0:T(1024)S(1)}, f32[1024]{0:T(1024)S(1)}, u32[]{:S(2)}, u32[]{:S(2)}) collective-permute-start(f32[1024]{0:T(1024)S(1)} %get-tuple-element.10), channel_id=1, source_target_pairs={{0,3},{1,4},{2,5},{3,6},{4,7},{5,8},{6,9},{7,10},{8,11},{9,12},{10... | collective-permute-start | bytes 12296 | tf_op jit(solution)/shard_map/ppermute | solution.py:14
  147.7 9.8 %collective-permute-start.7 = (f32[1024]{0:T(1024)S(1)}, f32[1024]{0:T(1024)S(1)}, u32[]{:S(2)}, u32[]{:S(2)}) collective-permute-start(f32[1024]{0:T(1024)S(1)} %get-tuple-element.13), channel_id=1, source_target_pairs={{0,2},{1,3},{2,4},{3,5},{4,6},{5,7},{6,8},{7,9},{8,10},{9,11},{10,... | collective-permute-start | bytes 12296 | tf_op jit(solution)/shard_map/ppermute | solution.py:14
  149.6 7.9 %collective-permute-start.3 = (f32[1024]{0:T(1024)S(1)}, f32[1024]{0:T(1024)S(1)}, u32[]{:S(2)}, u32[]{:S(2)}) collective-permute-start(f32[1024]{0:T(1024)S(1)} %get-tuple-element.11), channel_id=1, source_target_pairs={{0,1},{1,2},{2,3},{3,4},{4,5},{5,6},{6,7},{7,8},{8,9},{9,10},{10,1... | collective-permute-start | bytes 12296 | tf_op jit(solution)/shard_map/ppermute | solution.py:14
where the time goes:
time: 159 us; the launch traced here: 158 us
  starting transfers between devices  69.4 us (44%)
  waiting for transfers between devices  66.7 us (42%)
  matrix products  15.6 us (10%)
  other arithmetic  5.43 us (3%)
    ppermute x12, starting transfers between devices, from_behind(): lax.ppermute(array, axis, [(i, (i + by) % size) for i in range(size)])  69.4 us
    ppermute x12, waiting for transfers between devices, from_behind(): lax.ppermute(array, axis, [(i, (i + by) % size) for i in range(size)])  66.7 us
    dot_general x4, matrix products, cosines(): lax.dot_general(left, right, (((1,), (1,)), ((), ())), preferred_element_...  15.6 us
  transfers between devices with their start and end apart: 12, of which 3 were waited for; matrix products, arithmetic and copies ran while one was open for 7% of the time, Pallas kernels for 0%

commit v1 on v0

v1 whole, which is shorter than its diff:
```python
import functools

import jax
import jax.numpy as jnp
from jax import lax
from jax.experimental import pallas as pl
from jax.experimental.pallas import tpu as pltpu
from jax.sharding import PartitionSpec as P

MESH = pl.DeviceIdType.MESH
EPS = 1e-06
LOW = -3.0e38
XS = 4
CH = 256

A, B, LO, UP = 0, 1, 2, 3


def kernel(
    blocks, emb, ids, count, out,
    rows, relay, cmeta, rmeta, racc, cacc, vec, got,
    own_sem, sib_sem, up_send, up_recv, lo_send, lo_recv, via_send, via_recv, fwd_send,
    meta_send, meta_recv, vec_send, vec_recv,
):
    n, d = emb.shape
    chunks = n // CH
    half = chunks // 2
    mem = lax.axis_size("mem")
    zs = mem // (2 * 2)
    b = lax.axis_index("grp") * mem + lax.axis_index("mem")

    def device(i):
        i = lax.rem(i + blocks, blocks)
        return (i // mem, lax.rem(i, mem))

    def place(i):
        c = lax.rem(i + blocks, blocks) // 2
        return lax.rem(c // zs, XS), lax.rem(c, zs)

    core = lax.rem(b, 2)
    x, z = place(b)
    x_below, _ = place(b - 2)
    even, even_below = lax.rem(x, 2) == 0, lax.rem(x_below, 2) == 0
    first, second = core == 0, core == 1
    has_up = jnp.logical_or(first, even)
    has_lo = jnp.logical_or(first, jnp.logical_not(even_below))
    send_down = jnp.logical_or(first, even_below)
    send_up = jnp.logical_or(second, jnp.logical_not(even))
    sibling = b + 1 - 2 * core
    down, up = b - 2, b + 3 - 2 * core
    above, below = b + 2, b - 1 - 2 * core
    step = 2 * zs

    def flip(i):
        return i + step - 2 * step * lax.rem(place(i)[0], 2)

    via_down = jnp.logical_and(second, even_below)
    via_up = jnp.logical_and(first, jnp.logical_not(even))
    uses_via = jnp.logical_or(via_down, via_up)
    ring_up = jnp.where(x == XS - 1, b - (XS - 1) * step, b + step)
    ring_down = jnp.where(x == 0, b + (XS - 1) * step, b - step)
    last = z == zs - 1
    via = jnp.where(jnp.logical_and(first, last), ring_up, flip(b))
    is_relay = jnp.where(
        first, even, jnp.logical_or(jnp.logical_and(jnp.logical_not(even), z > 0), jnp.logical_and(even, z == 0))
    )
    relay_from = jnp.where(jnp.logical_and(first, last), ring_down, flip(b))
    relay_to = jnp.where(first, relay_from + 3, relay_from - 2)
    split_up = jnp.logical_and(second, has_up)
    split_lo = jnp.logical_and(second, has_lo)
    up_relay = flip(b + 2)
    lo_src = b - 3
    lo_x, lo_z = place(lo_src)
    lo_relay = jnp.where(
        lo_z == zs - 1, jnp.where(lo_x == XS - 1, lo_src - (XS - 1) * step, lo_src + step), flip(lo_src)
    )

    mine = pl.ds(pl.multiple_of(core * n, n), n)
    own = pltpu.make_async_copy(emb, rows.at[mine], own_sem)
    own.start()

    barrier = pltpu.get_barrier_semaphore()

    def greet(i):
        pl.semaphore_signal(barrier, inc=1, device_id=device(i), device_id_type=MESH)

    for i in (sibling, down, up, above, below):
        greet(i)
    pl.when(is_relay)(lambda: greet(relay_from))
    pl.when(split_up)(lambda: greet(up_relay))
    pl.when(split_lo)(lambda: greet(lo_relay))
    pl.semaphore_wait(barrier, 5 + uses_via.astype(jnp.int32) + is_relay.astype(jnp.int32))

    def copy(src, dst, send, recv, to):
        return pltpu.make_async_remote_copy(
            src_ref=src, dst_ref=dst, send_sem=send, recv_sem=recv, device_id=device(to), device_id_type=MESH
        )

    def part(slot, k):
        return pl.ds(slot * n + k * CH, CH)

    def emb_part(k):
        return emb.at[pl.ds(k * CH, CH)]

    swap = copy(emb, rows.at[mine], sib_sem.at[0], sib_sem.at[1], sibling)
    swap.start()
    downs = [copy(emb_part(k), rows.at[part(UP, k)], up_send.at[k], up_recv.at[k], down) for k in range(chunks)]
    ups = [copy(emb_part(k), rows.at[part(LO, k)], lo_send.at[k], lo_recv.at[k], up) for k in range(chunks)]
    vias = [
        copy(emb_part(half + k), relay.at[pl.ds(k * CH, CH)], via_send.at[k], via_recv.at[k], via) for k in range(half)
    ]
    fwd_up = [
        copy(relay.at[pl.ds(k * CH, CH)], rows.at[part(LO, half + k)], fwd_send.at[k], lo_recv.at[half + k], relay_to)
        for k in range(half)
    ]
    fwd_down = [
        copy(relay.at[pl.ds(k * CH, CH)], rows.at[part(UP, half + k)], fwd_send.at[k], up_recv.at[half + k], relay_to)
        for k in range(half)
    ]
    whole_down = jnp.logical_and(send_down, first)
    whole_up = jnp.logical_and(send_up, second)

    for k in range(half):
        pl.when(uses_via)(vias[k].start)
    for k in range(chunks):
        pl.when(send_down if k < half else whole_down)(downs[k].start)
        pl.when(send_up if k < half else whole_up)(ups[k].start)

    own.wait()
    cacc[...] = jnp.full(cacc.shape, LOW, jnp.float32)
    racc[...] = jnp.full(racc.shape, LOW, jnp.float32)
    lanes = lax.broadcasted_iota(jnp.int32, (1, n), 1)
    own_ids = ids[...].astype(jnp.float32)
    valid_ids = jnp.where(lanes < count[0], own_ids, -1.0)
    cmeta[1:2, mine] = own_ids
    cmeta[2:3, mine] = valid_ids

    def squares(t, _):
        at = pl.ds(pl.multiple_of(core * n + t * 128, 128), 128)
        block = rows[at, :].astype(jnp.float32)
        scale = lax.rsqrt(jnp.sum(block * block, axis=1, keepdims=True) + EPS)
        wide = jnp.broadcast_to(scale, (128, 128))
        cmeta[0:1, at] = wide.T[0:1]
        return 0

    lax.fori_loop(0, n // 128, squares, 0)

    def spread(slot):
        def group(t, _):
            at = pl.ds(pl.multiple_of(slot * n + t * 128, 128), 128)
            for j in range(3):
                rmeta[j, at, :] = jnp.broadcast_to(cmeta[j : j + 1, at], (128, 128)).T
            return 0

        lax.fori_loop(0, n // 128, group, 0)

    def meta(slot):
        return cmeta.at[:, pl.ds(slot * n, n)]

    meta_sib = copy(cmeta.at[:, mine], cmeta.at[:, mine], meta_send.at[0], meta_recv.at[0], sibling)
    meta_down = copy(cmeta.at[:, mine], meta(UP), meta_send.at[1], meta_recv.at[1], down)
    meta_up = copy(cmeta.at[:, mine], meta(LO), meta_send.at[2], meta_recv.at[2], up)
    meta_sib.start()
    pl.when(send_down)(meta_down.start)
    pl.when(send_up)(meta_up.start)
    spread(core)

    def cosines(row, col, masked_diagonal):
        return lax.dot_general(
            rows[pl.ds(row, CH), :], rows[pl.ds(col, CH), :], (((1,), (1,)), ((), ())),
            preferred_element_type=jnp.float32,
        )

    def fold(values):
        return jnp.max(values.reshape(CH // 8, 8, 128), axis=0)

    def run(col, row, tiles):
        col = pl.multiple_of(col, CH)

        def tile(t, best):
            at = pl.multiple_of(row + t * CH, CH)
            dots = cosines(at, col, False)
            at = pl.ds(at, CH)
            scale, own_id, own_valid = rmeta[0, at, :], rmeta[1, at, :], rmeta[2, at, :]
            row_best = racc[at, :]
            out_best = []
            for h in range(CH // 128):
                lane = pl.ds(pl.multiple_of(col + h * 128, 128), 128)
                dot = dots[:, h * 128 : (h + 1) * 128]
                row_best = jnp.maximum(
                    row_best, jnp.where(own_id == cmeta[2:3, lane], dot * cmeta[0:1, lane], LOW)
                )
                out_best.append(
                    jnp.maximum(best[h], fold(jnp.where(own_valid == cmeta[1:2, lane], dot * scale, LOW)))
                )
            racc[at, :] = row_best
            return tuple(out_best)

        def lanes_of(h):
            return pl.ds(pl.multiple_of(col + h * 128, 128), 128)

        start = tuple(cacc[:, lanes_of(h)] for h in range(CH // 128))
        end = lax.fori_loop(0, tiles, tile, start)
        for h in range(CH // 128):
            cacc[:, lanes_of(h)] = end[h]

    def run_self(col, row):
        col = pl.multiple_of(col, CH)

        def tile(t, best):
            first_row = pl.multiple_of(row + t * CH, CH)
            dots = cosines(first_row, col, True)
            at = pl.ds(first_row, CH)
            scale, own_valid = rmeta[0, at, :], rmeta[2, at, :]
            apart = lax.broadcasted_iota(jnp.int32, (CH, 128), 1) - lax.broadcasted_iota(jnp.int32, (CH, 128), 0)
            out_best = []
            for h in range(CH // 128):
                lane = pl.ds(pl.multiple_of(col + h * 128, 128), 128)
                dot = dots[:, h * 128 : (h + 1) * 128]
                keep = jnp.logical_and(own_valid == cmeta[1:2, lane], apart != first_row - col - h * 128)
                out_best.append(jnp.maximum(best[h], fold(jnp.where(keep, dot * scale, LOW))))
            return tuple(out_best)

        start = tuple(jnp.full((8, 128), LOW, jnp.float32) for _ in range(CH // 128))
        end = lax.fori_loop(0, n // CH, tile, start)
        for h in range(CH // 128):
            cacc[:, pl.ds(pl.multiple_of(col + h * 128, 128), 128)] = end[h]

    def own_chunk(k, _):
        run_self(core * n + k * CH, core * n)
        return 0

    lax.fori_loop(0, chunks, own_chunk, 0)

    meta_sib.wait_recv()
    theirs = pl.ds(pl.multiple_of(n - core * n, n), n)
    copy(emb, rows.at[theirs], sib_sem.at[0], sib_sem.at[1], sibling).wait_recv()
    spread(1 - core)

    def sibling_chunk(k, _):
        run(B * n + k * CH, A * n, core * chunks)
        return 0

    lax.fori_loop(0, chunks, sibling_chunk, 0)

    pl.when(has_up)(meta_down.wait_recv)
    pl.when(has_up)(lambda: spread(UP))
    pl.when(has_lo)(meta_up.wait_recv)
    pl.when(has_lo)(lambda: spread(LO))

    zero = core * 0
    for k in range(chunks):
        if k < half:

            @pl.when(is_relay)
            def _():
                vias[k].wait_recv()

            pl.when(jnp.logical_and(is_relay, first))(fwd_up[k].start)
            pl.when(jnp.logical_and(is_relay, second))(fwd_down[k].start)
        pl.when(has_up)(downs[k].wait_recv)
        pl.when(has_lo)(ups[k].wait_recv)
        run(UP * n + k * CH, A * n, jnp.where(first, 2 * chunks + k, jnp.where(has_up, 2 * chunks, zero)))
        run(LO * n + k * CH, UP * n, jnp.where(first, k + 1, zero))
        run(LO * n + k * CH, B * n, jnp.where(even_below, zero, chunks))

    def finish(slot):
        def group(t, _):
            at = pl.ds(pl.multiple_of(slot * n + t * 128, 128), 128)
            best = jnp.maximum(
                jnp.max(racc[at, :].T, axis=0, keepdims=True), jnp.max(cacc[:, at], axis=0, keepdims=True)
            )
            vec[slot, pl.ds(t, 1), :] = best * cmeta[0:1, at]
            return 0

        lax.fori_loop(0, n // 128, group, 0)

    send_vec_up = copy(vec.at[UP], got.at[1], vec_send.at[1], vec_recv.at[1], above)
    send_vec_lo = copy(vec.at[LO], got.at[2], vec_send.at[2], vec_recv.at[2], below)
    send_vec_sib = copy(vec.at[1 - core], got.at[0], vec_send.at[0], vec_recv.at[0], sibling)

    @pl.when(has_up)
    def _():
        finish(UP)
        send_vec_up.start()

    @pl.when(has_lo)
    def _():
        finish(LO)
        send_vec_lo.start()

    finish(1 - core)
    send_vec_sib.start()
    finish(core)
    best = jnp.maximum(vec[core], -2.0)
    got_down, got_up = send_down, send_up
    send_vec_sib.wait_recv()
    best = jnp.maximum(best, got[0])
    out[...] = best

    @pl.when(got_down)
    def _():
        send_vec_up.wait_recv()
        out[...] = jnp.maximum(out[...], got[1])

    @pl.when(got_up)
    def _():
        send_vec_lo.wait_recv()
        out[...] = jnp.maximum(out[...], got[2])

    swap.wait_send()
    meta_sib.wait_send()
    send_vec_sib.wait_send()
    pl.when(send_down)(meta_down.wait_send)
    pl.when(send_up)(meta_up.wait_send)
    pl.when(has_up)(send_vec_up.wait_send)
    pl.when(has_lo)(send_vec_lo.wait_send)
    for k in range(half):
        pl.when(uses_via)(vias[k].wait_send)
        pl.when(is_relay)(fwd_up[k].wait_send)
    for k in range(chunks):
        pl.when(send_down if k < half else whole_down)(downs[k].wait_send)
        pl.when(send_up if k < half else whole_up)(ups[k].wait_send)


def shards(blocks, embeddings, cluster_ids, valid_counts):
    n, d = embeddings.shape
    chunks = n // CH
    dma = pltpu.SemaphoreType.DMA
    best = pl.pallas_call(
        functools.partial(kernel, blocks),
        out_shape=jax.ShapeDtypeStruct((n // 128, 128), jnp.float32),
        in_specs=[
            pl.BlockSpec(memory_space=pl.ANY),
            pl.BlockSpec(memory_space=pltpu.VMEM),
            pl.BlockSpec(memory_space=pltpu.SMEM),
        ],
        out_specs=pl.BlockSpec(memory_space=pltpu.VMEM),
        scratch_shapes=[
            pltpu.VMEM((4 * n, d), jnp.bfloat16),
            pltpu.VMEM((n // 2, d), jnp.bfloat16),
            pltpu.VMEM((8, 4 * n), jnp.float32),
            pltpu.VMEM((3, 4 * n, 128), jnp.float32),
            pltpu.VMEM((4 * n, 128), jnp.float32),
            pltpu.VMEM((8, 4 * n), jnp.float32),
            pltpu.VMEM((4, n // 128, 128), jnp.float32),
            pltpu.VMEM((3, n // 128, 128), jnp.float32),
            dma(()), dma((2,)),
            dma((chunks,)), dma((chunks,)), dma((chunks,)), dma((chunks,)),
            dma((chunks // 2,)), dma((chunks // 2,)), dma((chunks // 2,)),
            dma((3,)), dma((3,)), dma((3,)), dma((3,)),
        ],
        compiler_params=pltpu.CompilerParams(
            collective_id=0, has_side_effects=True, vmem_limit_bytes=56 * 2**20
        ),
        name="neighbour_cosines",
    )(embeddings, cluster_ids.reshape(1, n), valid_counts)
    return best.reshape(n)


def solution(mesh):
    placed = (P(("grp", "mem"), None), P(("grp", "mem")), P(("grp", "mem")))
    return jax.shard_map(
        functools.partial(shards, mesh.size),
        mesh=mesh, in_specs=placed, out_specs=P(("grp", "mem")), check_vma=False,
    )
```

time: 159 us -> 74.9 us (0.47)
  Pallas kernels: 0 us -> 72.8 us
  starting transfers between devices: 69.4 us -> 0 us
  waiting for transfers between devices: 66.7 us -> 0 us
  matrix products: 15.6 us -> 0 us
  other arithmetic: 5.43 us -> 0 us
    pallas_call x0 -> x1, Pallas kernels: none -> 72.8 us  [shards(): pl.pallas_call(functools.partial(kernel, blocks), out_shape=jax.ShapeDtyp...]
    ppermute x12 -> x0, starting transfers between devices: 69.4 us -> none  [from_behind(): lax.ppermute(array, axis, [(i, (i + by) % size) for i in range(size)])]
    ppermute x12 -> x0, waiting for transfers between devices: 66.7 us -> none  [from_behind(): lax.ppermute(array, axis, [(i, (i + by) % size) for i in range(size)])]
    dot_general x4 -> x0, matrix products: 15.6 us -> none  [cosines(): lax.dot_general(left, right, (((1,), (1,)), ((), ())), preferred_element_...]
    reduce_sum x4 -> x0, other arithmetic: 2.91 us -> none  [row_scale(): jnp.sum(jnp.square(block.astype(jnp.float32)), axis=1) + EPS]
    lt x4 -> x0, other arithmetic: 1.9 us -> none  [the longest x3 1.9 us: shards(): upper_valid = positions < upper_count[0]]
  transfers between devices with their start and end apart: 12 -> 0, of which waited for: 3 -> 0; matrix products, arithmetic and copies ran while one was open for 7% -> 0% of each run, Pallas kernels for 0% -> 0%
where the time goes in v1:
time: 74.9 us; the launch traced here: 74.7 us
  Pallas kernels  72.8 us (97%)
  local copies, waits for them, and re-layouts  1.28 us (2%)
    pallas_call x1, Pallas kernels, shards(): pl.pallas_call(functools.partial(kernel, blocks), out_shape=jax.ShapeDtyp...  72.8 us

profile of v1, /device:TPU:1, one launch (start us, length us, event | category | flops | bytes accessed | tf_op | source)
XLA Modules:
  0.0 74.7 jit_solution(13034883934243568269)
XLA Ops:
  0.7 72.8 %neighbour_cosines.1 = f32[8,128]{1,0:T(8,128)} custom-call(bf16[1024,768]{1,0:T(8,128)(2,1)} %emb.1, s32[1,1024]{1,0:T(1,128)} %bitcast.3, s32[1]{0:T(128)S(6)} %copy.5.count), custom_call_target="tpu_custom_call" | custom-call | tf_op jit(solution)/shard_map/neighbour_cosines/pallas_call | solution.py:330
  73.4 1.3 %copy.6 = f32[1024]{0:T(1024)} copy(f32[1024]{0:T(1024)} %bitcast.2) | data formatting | bytes 8192

commit v2 on v1

--- a/solution.py
+++ b/solution.py
@@ -38,42 +38,47 @@
         return lax.rem(c // zs, XS), lax.rem(c, zs)
 
     core = lax.rem(b, 2)
-    x, z = place(b)
-    x_below, _ = place(b - 2)
-    even, even_below = lax.rem(x, 2) == 0, lax.rem(x_below, 2) == 0
     first, second = core == 0, core == 1
-    has_up = jnp.logical_or(first, even)
-    has_lo = jnp.logical_or(first, jnp.logical_not(even_below))
-    send_down = jnp.logical_or(first, even_below)
-    send_up = jnp.logical_or(second, jnp.logical_not(even))
+    step = 2 * zs
+
+    def goes_down(i):
+        x, z = place(i)
+        return (lax.rem(x, 2) == 0) != (z == 0)
+
+    def next_x(i):
+        return jnp.where(place(i)[0] == XS - 1, i - (XS - 1) * step, i + step)
+
+    def last_x(i):
+        return jnp.where(place(i)[0] == 0, i + (XS - 1) * step, i - step)
+
+    def relay_down(i):
+        return jnp.where(place(i)[1] == 0, last_x(i), next_x(i))
+
+    def relay_up(i):
+        return jnp.where(place(i)[1] == zs - 1, next_x(i), last_x(i))
+
+    up_down, lo_down = goes_down(b), goes_down(b - 2)
+    has_up = jnp.logical_or(first, up_down)
+    has_lo = jnp.logical_or(first, jnp.logical_not(lo_down))
+    send_down = jnp.logical_or(first, lo_down)
+    send_up = jnp.logical_or(second, jnp.logical_not(up_down))
     sibling = b + 1 - 2 * core
     down, up = b - 2, b + 3 - 2 * core
     above, below = b + 2, b - 1 - 2 * core
-    step = 2 * zs
-
-    def flip(i):
-        return i + step - 2 * step * lax.rem(place(i)[0], 2)
-
-    via_down = jnp.logical_and(second, even_below)
-    via_up = jnp.logical_and(first, jnp.logical_not(even))
+
+    via_down = jnp.logical_and(second, lo_down)
+    via_up = jnp.logical_and(first, jnp.logical_not(up_down))
     uses_via = jnp.logical_or(via_down, via_up)
-    ring_up = jnp.where(x == XS - 1, b - (XS - 1) * step, b + step)
-    ring_down = jnp.where(x == 0, b + (XS - 1) * step, b - step)
-    last = z == zs - 1
-    via = jnp.where(jnp.logical_and(first, last), ring_up, flip(b))
-    is_relay = jnp.where(
-        first, even, jnp.logical_or(jnp.logical_and(jnp.logical_not(even), z > 0), jnp.logical_and(even, z == 0))
+    via = jnp.where(first, relay_up(b), relay_down(b))
+    z = place(b)[1]
+    relay_from = jnp.where(
+        jnp.where(first, z == zs - 1, z != 0), last_x(b), next_x(b)
     )
-    relay_from = jnp.where(jnp.logical_and(first, last), ring_down, flip(b))
+    is_relay = jnp.where(first, jnp.logical_not(goes_down(relay_from)), goes_down(relay_from - 2))
     relay_to = jnp.where(first, relay_from + 3, relay_from - 2)
     split_up = jnp.logical_and(second, has_up)
     split_lo = jnp.logical_and(second, has_lo)
-    up_relay = flip(b + 2)
-    lo_src = b - 3
-    lo_x, lo_z = place(lo_src)
-    lo_relay = jnp.where(
-        lo_z == zs - 1, jnp.where(lo_x == XS - 1, lo_src - (XS - 1) * step, lo_src + step), flip(lo_src)
-    )
+    up_relay, lo_relay = relay_down(b + 2), relay_up(b - 3)
 
     mine = pl.ds(pl.multiple_of(core * n, n), n)
     own = pltpu.make_async_copy(emb, rows.at[mine], own_sem)
@@ -97,10 +102,10 @@
         )
 
     def part(slot, k):
-        return pl.ds(slot * n + k * CH, CH)
+        return pl.ds(pl.multiple_of(slot * n + k * CH, CH), CH)
 
     def emb_part(k):
-        return emb.at[pl.ds(k * CH, CH)]
+        return emb.at[pl.ds(pl.multiple_of(k * CH, CH), CH)]
 
     swap = copy(emb, rows.at[mine], sib_sem.at[0], sib_sem.at[1], sibling)
     swap.start()
@@ -117,14 +122,21 @@
         copy(relay.at[pl.ds(k * CH, CH)], rows.at[part(UP, half + k)], fwd_send.at[k], up_recv.at[half + k], relay_to)
         for k in range(half)
     ]
-    whole_down = jnp.logical_and(send_down, first)
-    whole_up = jnp.logical_and(send_up, second)
-
-    for k in range(half):
-        pl.when(uses_via)(vias[k].start)
-    for k in range(chunks):
-        pl.when(send_down if k < half else whole_down)(downs[k].start)
-        pl.when(send_up if k < half else whole_up)(ups[k].start)
+    def send(k):
+        if k < half:
+            pl.when(uses_via)(vias[k].start)
+        pl.when(first)(downs[k].start)
+        pl.when(second)(ups[k].start)
+        if k < half:
+            pl.when(via_down)(downs[k].start)
+            pl.when(via_up)(ups[k].start)
+
+    send(0)
+
+    def forward(k):
+        pl.when(is_relay)(vias[k].wait_recv)
+        pl.when(jnp.logical_and(is_relay, first))(fwd_up[k].start)
+        pl.when(jnp.logical_and(is_relay, second))(fwd_down[k].start)
 
     own.wait()
     cacc[...] = jnp.full(cacc.shape, LOW, jnp.float32)
@@ -163,71 +175,48 @@
     meta_sib.start()
     pl.when(send_down)(meta_down.start)
     pl.when(send_up)(meta_up.start)
+    for k in range(1, chunks):
+        send(k)
     spread(core)
 
-    def cosines(row, col, masked_diagonal):
+    def dots(row, col):
         return lax.dot_general(
-            rows[pl.ds(row, CH), :], rows[pl.ds(col, CH), :], (((1,), (1,)), ((), ())),
+            rows[pl.ds(row, n), :], rows[pl.ds(col, CH), :], (((1,), (1,)), ((), ())),
             preferred_element_type=jnp.float32,
         )
 
     def fold(values):
-        return jnp.max(values.reshape(CH // 8, 8, 128), axis=0)
-
-    def run(col, row, tiles):
-        col = pl.multiple_of(col, CH)
-
-        def tile(t, best):
-            at = pl.multiple_of(row + t * CH, CH)
-            dots = cosines(at, col, False)
-            at = pl.ds(at, CH)
-            scale, own_id, own_valid = rmeta[0, at, :], rmeta[1, at, :], rmeta[2, at, :]
-            row_best = racc[at, :]
-            out_best = []
-            for h in range(CH // 128):
-                lane = pl.ds(pl.multiple_of(col + h * 128, 128), 128)
-                dot = dots[:, h * 128 : (h + 1) * 128]
-                row_best = jnp.maximum(
-                    row_best, jnp.where(own_id == cmeta[2:3, lane], dot * cmeta[0:1, lane], LOW)
-                )
-                out_best.append(
-                    jnp.maximum(best[h], fold(jnp.where(own_valid == cmeta[1:2, lane], dot * scale, LOW)))
-                )
-            racc[at, :] = row_best
-            return tuple(out_best)
-
-        def lanes_of(h):
-            return pl.ds(pl.multiple_of(col + h * 128, 128), 128)
-
-        start = tuple(cacc[:, lanes_of(h)] for h in range(CH // 128))
-        end = lax.fori_loop(0, tiles, tile, start)
+        return jnp.max(values.reshape(n // 8, 8, 128), axis=0)
+
+    def lanes_of(col, h):
+        return pl.ds(pl.multiple_of(col + h * 128, 128), 128)
+
+    def pair(col, row):
+        col, row = pl.multiple_of(col, CH), pl.multiple_of(row, n)
+        dot = dots(row, col)
+        at = pl.ds(row, n)
+        scale, own_id, own_valid = rmeta[0, at, :], rmeta[1, at, :], rmeta[2, at, :]
+        row_best = racc[at, :]
         for h in range(CH // 128):
-            cacc[:, lanes_of(h)] = end[h]
-
-    def run_self(col, row):
-        col = pl.multiple_of(col, CH)
-
-        def tile(t, best):
-            first_row = pl.multiple_of(row + t * CH, CH)
-            dots = cosines(first_row, col, True)
-            at = pl.ds(first_row, CH)
-            scale, own_valid = rmeta[0, at, :], rmeta[2, at, :]
-            apart = lax.broadcasted_iota(jnp.int32, (CH, 128), 1) - lax.broadcasted_iota(jnp.int32, (CH, 128), 0)
-            out_best = []
-            for h in range(CH // 128):
-                lane = pl.ds(pl.multiple_of(col + h * 128, 128), 128)
-                dot = dots[:, h * 128 : (h + 1) * 128]
-                keep = jnp.logical_and(own_valid == cmeta[1:2, lane], apart != first_row - col - h * 128)
-                out_best.append(jnp.maximum(best[h], fold(jnp.where(keep, dot * scale, LOW))))
-            return tuple(out_best)
-
-        start = tuple(jnp.full((8, 128), LOW, jnp.float32) for _ in range(CH // 128))
-        end = lax.fori_loop(0, n // CH, tile, start)
+            lane = lanes_of(col, h)
+            d = dot[:, h * 128 : (h + 1) * 128]
+            row_best = jnp.maximum(row_best, jnp.where(own_id == cmeta[2:3, lane], d * cmeta[0:1, lane], LOW))
+            col_best = fold(jnp.where(own_valid == cmeta[1:2, lane], d * scale, LOW))
+            cacc[:, lane] = jnp.maximum(cacc[:, lane], col_best)
+        racc[at, :] = row_best
+
+    def own_chunk(k, _):
+        row = pl.multiple_of(core * n, n)
+        col = pl.multiple_of(row + k * CH, CH)
+        dot = dots(row, col)
+        at = pl.ds(row, n)
+        scale, own_valid = rmeta[0, at, :], rmeta[2, at, :]
+        apart = lax.broadcasted_iota(jnp.int32, (n, 128), 0) - lax.broadcasted_iota(jnp.int32, (n, 128), 1)
         for h in range(CH // 128):
-            cacc[:, pl.ds(pl.multiple_of(col + h * 128, 128), 128)] = end[h]
-
-    def own_chunk(k, _):
-        run_self(core * n + k * CH, core * n)
+            lane = lanes_of(col, h)
+            d = dot[:, h * 128 : (h + 1) * 128]
+            keep = jnp.logical_and(own_valid == cmeta[1:2, lane], apart != k * CH + h * 128)
+            cacc[:, lane] = fold(jnp.where(keep, d * scale, LOW))
         return 0
 
     lax.fori_loop(0, chunks, own_chunk, 0)
@@ -237,43 +226,55 @@
     copy(emb, rows.at[theirs], sib_sem.at[0], sib_sem.at[1], sibling).wait_recv()
     spread(1 - core)
 
-    def sibling_chunk(k, _):
-        run(B * n + k * CH, A * n, core * chunks)
+    for k in range(half):
+        forward(k)
+
+    end = chunks + 1
+
+    def stage(e, _):
+        arrival = jnp.logical_and(e >= 1, e < end)
+        k = jnp.where(first, e - 1, lax.rem(e - 1 + chunks, 2) * half + (e - 1 + chunks) // 2 - half)
+        k = jnp.clip(k, 0, chunks - 1)
+
+        @pl.when(e == 1)
+        def _():
+            pl.when(has_up)(meta_down.wait_recv)
+            pl.when(has_up)(lambda: spread(UP))
+            pl.when(has_lo)(meta_up.wait_recv)
+            pl.when(has_lo)(lambda: spread(LO))
+
+        @pl.when(jnp.logical_and(arrival, has_up))
+        def _():
+            copy(emb_part(k), rows.at[part(UP, k)], up_send.at[k], up_recv.at[k], down).wait_recv()
+
+        @pl.when(jnp.logical_and(arrival, has_lo))
+        def _():
+            copy(emb_part(k), rows.at[part(LO, k)], lo_send.at[k], lo_recv.at[k], up).wait_recv()
+
+        def unit(j, _):
+            slot = jnp.where(j < 2, UP, LO)
+            col = jnp.where(arrival, slot * n + k * CH, jnp.where(e == 0, B, LO) * n + j * CH)
+            row = jnp.where(arrival, jnp.where(j == 0, A, B), jnp.where(e == 0, A, UP))
+            wanted = jnp.where(
+                arrival,
+                jnp.where(j < 2, has_up, jnp.logical_and(j == 2, jnp.logical_not(lo_down))).astype(jnp.int32),
+                jnp.where(e == 0, second, first).astype(jnp.int32),
+            )
+            pl.when(wanted == 1)(lambda: pair(col, row * n))
+            return 0
+
+        lax.fori_loop(0, chunks, unit, 0)
         return 0
 
-    lax.fori_loop(0, chunks, sibling_chunk, 0)
-
-    pl.when(has_up)(meta_down.wait_recv)
-    pl.when(has_up)(lambda: spread(UP))
-    pl.when(has_lo)(meta_up.wait_recv)
-    pl.when(has_lo)(lambda: spread(LO))
-
-    zero = core * 0
-    for k in range(chunks):
-        if k < half:
-
-            @pl.when(is_relay)
-            def _():
-                vias[k].wait_recv()
-
-            pl.when(jnp.logical_and(is_relay, first))(fwd_up[k].start)
-            pl.when(jnp.logical_and(is_relay, second))(fwd_down[k].start)
-        pl.when(has_up)(downs[k].wait_recv)
-        pl.when(has_lo)(ups[k].wait_recv)
-        run(UP * n + k * CH, A * n, jnp.where(first, 2 * chunks + k, jnp.where(has_up, 2 * chunks, zero)))
-        run(LO * n + k * CH, UP * n, jnp.where(first, k + 1, zero))
-        run(LO * n + k * CH, B * n, jnp.where(even_below, zero, chunks))
+    lax.fori_loop(0, end + 1, stage, 0)
 
     def finish(slot):
-        def group(t, _):
+        for t in range(n // 128):
             at = pl.ds(pl.multiple_of(slot * n + t * 128, 128), 128)
             best = jnp.maximum(
                 jnp.max(racc[at, :].T, axis=0, keepdims=True), jnp.max(cacc[:, at], axis=0, keepdims=True)
             )
-            vec[slot, pl.ds(t, 1), :] = best * cmeta[0:1, at]
-            return 0
-
-        lax.fori_loop(0, n // 128, group, 0)
+            vec[slot, t : t + 1, :] = best * cmeta[0:1, at]
 
     send_vec_up = copy(vec.at[UP], got.at[1], vec_send.at[1], vec_recv.at[1], above)
     send_vec_lo = copy(vec.at[LO], got.at[2], vec_send.at[2], vec_recv.at[2], below)
@@ -319,8 +320,8 @@
         pl.when(uses_via)(vias[k].wait_send)
         pl.when(is_relay)(fwd_up[k].wait_send)
     for k in range(chunks):
-        pl.when(send_down if k < half else whole_down)(downs[k].wait_send)
-        pl.when(send_up if k < half else whole_up)(ups[k].wait_send)
+        pl.when(send_down if k < half else first)(downs[k].wait_send)
+        pl.when(send_up if k < half else second)(ups[k].wait_send)
 
 
 def shards(blocks, embeddings, cluster_ids, valid_counts):

time: 74.9 us -> 55.4 us (0.74)
  Pallas kernels: 72.8 us -> 53.3 us
    pallas_call x1, Pallas kernels: 72.8 us -> 53.3 us  [shards(): pl.pallas_call(functools.partial(kernel, blocks), out_shape=jax.ShapeDtyp...]
where the time goes in v2:
time: 55.4 us; the launch traced here: 55.2 us
  Pallas kernels  53.3 us (96%)
  local copies, waits for them, and re-layouts  1.28 us (2%)
  between operations  0.66 us (1%)
    pallas_call x1, Pallas kernels, shards(): pl.pallas_call(functools.partial(kernel, blocks), out_shape=jax.ShapeDtyp...  53.3 us
    unnamed x1, local copies, waits for them, and re-layouts  1.28 us

profile of v2, /device:TPU:1, one launch (start us, length us, event | category | flops | bytes accessed | tf_op | source)
XLA Modules:
  0.0 55.2 jit_solution(15547324464063116242)
XLA Ops:
  0.7 53.3 %neighbour_cosines.1 = f32[8,128]{1,0:T(8,128)} custom-call(bf16[1024,768]{1,0:T(8,128)(2,1)} %emb.1, s32[1,1024]{1,0:T(1,128)} %bitcast.3, s32[1]{0:T(128)S(6)} %copy.5.count), custom_call_target="tpu_custom_call" | custom-call | tf_op jit(solution)/shard_map/neighbour_cosines/pallas_call | solution.py:331
  53.9 1.3 %copy.6 = f32[1024]{0:T(1024)} copy(f32[1024]{0:T(1024)} %bitcast.2) | data formatting | bytes 8192

commit v3 on v2

--- a/solution.py
+++ b/solution.py
@@ -11,6 +11,7 @@
 EPS = 1e-06
 LOW = -3.0e38
 XS = 4
+WAIT_B, STAGE_A = 2, 3
 CH = 256
 
 A, B, LO, UP = 0, 1, 2, 3
@@ -127,7 +128,9 @@
             pl.when(uses_via)(vias[k].start)
         pl.when(first)(downs[k].start)
         pl.when(second)(ups[k].start)
-        if k < half:
+
+    def send_third():
+        for k in range(half):
             pl.when(via_down)(downs[k].start)
             pl.when(via_up)(ups[k].start)
 
@@ -226,9 +229,6 @@
     copy(emb, rows.at[theirs], sib_sem.at[0], sib_sem.at[1], sibling).wait_recv()
     spread(1 - core)
 
-    for k in range(half):
-        forward(k)
-
     end = chunks + 1
 
     def stage(e, _):
@@ -242,6 +242,19 @@
             pl.when(has_up)(lambda: spread(UP))
             pl.when(has_lo)(meta_up.wait_recv)
             pl.when(has_lo)(lambda: spread(LO))
+
+            @pl.when(second)
+            def _():
+                ups[WAIT_B].wait_send()
+                send_third()
+                for j in range(half):
+                    forward(j)
+
+        @pl.when(jnp.logical_and(first, e == STAGE_A))
+        def _():
+            send_third()
+            for j in range(half):
+                forward(j)
 
         @pl.when(jnp.logical_and(arrival, has_up))
         def _():
@@ -321,7 +334,11 @@
         pl.when(is_relay)(fwd_up[k].wait_send)
     for k in range(chunks):
         pl.when(send_down if k < half else first)(downs[k].wait_send)
-        pl.when(send_up if k < half else second)(ups[k].wait_send)
+        if k == WAIT_B:
+            if k < half:
+                pl.when(via_up)(ups[k].wait_send)
+        else:
+            pl.when(send_up if k < half else second)(ups[k].wait_send)
 
 
 def shards(blocks, embeddings, cluster_ids, valid_counts):

time: 55.4 us -> 52.5 us (0.948)
  Pallas kernels: 53.3 us -> 50.4 us
    pallas_call x1, Pallas kernels: 53.3 us -> 50.4 us  [shards(): pl.pallas_call(functools.partial(kernel, blocks), out_shape=jax.ShapeDtyp...]
where the time goes in v3:
time: 52.5 us; the launch traced here: 52.3 us
  Pallas kernels  50.4 us (96%)
  local copies, waits for them, and re-layouts  1.28 us (2%)
  between operations  0.66 us (1%)
    pallas_call x1, Pallas kernels, shards(): pl.pallas_call(functools.partial(kernel, blocks), out_shape=jax.ShapeDtyp...  50.4 us
    unnamed x1, local copies, waits for them, and re-layouts  1.28 us

profile of v3, /device:TPU:1, one launch (start us, length us, event | category | flops | bytes accessed | tf_op | source)
XLA Modules:
  0.0 52.3 jit_solution(4968023149089381197)
XLA Ops:
  0.7 50.4 %neighbour_cosines.1 = f32[8,128]{1,0:T(8,128)} custom-call(bf16[1024,768]{1,0:T(8,128)(2,1)} %emb.1, s32[1,1024]{1,0:T(1,128)} %bitcast.3, s32[1]{0:T(128)S(6)} %copy.5.count), custom_call_target="tpu_custom_call" | custom-call | tf_op jit(solution)/shard_map/neighbour_cosines/pallas_call | solution.py:348
  51.0 1.3 %copy.6 = f32[1024]{0:T(1024)} copy(f32[1024]{0:T(1024)} %bitcast.2) | data formatting | bytes 8192

commit v4 on v3

--- a/solution.py
+++ b/solution.py
@@ -90,6 +90,7 @@
     def greet(i):
         pl.semaphore_signal(barrier, inc=1, device_id=device(i), device_id_type=MESH)
 
+    low, high = z == 0, z == zs - 1
     for i in (sibling, down, up, above, below):
         greet(i)
     pl.when(is_relay)(lambda: greet(relay_from))
@@ -229,58 +230,6 @@
     copy(emb, rows.at[theirs], sib_sem.at[0], sib_sem.at[1], sibling).wait_recv()
     spread(1 - core)
 
-    end = chunks + 1
-
-    def stage(e, _):
-        arrival = jnp.logical_and(e >= 1, e < end)
-        k = jnp.where(first, e - 1, lax.rem(e - 1 + chunks, 2) * half + (e - 1 + chunks) // 2 - half)
-        k = jnp.clip(k, 0, chunks - 1)
-
-        @pl.when(e == 1)
-        def _():
-            pl.when(has_up)(meta_down.wait_recv)
-            pl.when(has_up)(lambda: spread(UP))
-            pl.when(has_lo)(meta_up.wait_recv)
-            pl.when(has_lo)(lambda: spread(LO))
-
-            @pl.when(second)
-            def _():
-                ups[WAIT_B].wait_send()
-                send_third()
-                for j in range(half):
-                    forward(j)
-
-        @pl.when(jnp.logical_and(first, e == STAGE_A))
-        def _():
-            send_third()
-            for j in range(half):
-                forward(j)
-
-        @pl.when(jnp.logical_and(arrival, has_up))
-        def _():
-            copy(emb_part(k), rows.at[part(UP, k)], up_send.at[k], up_recv.at[k], down).wait_recv()
-
-        @pl.when(jnp.logical_and(arrival, has_lo))
-        def _():
-            copy(emb_part(k), rows.at[part(LO, k)], lo_send.at[k], lo_recv.at[k], up).wait_recv()
-
-        def unit(j, _):
-            slot = jnp.where(j < 2, UP, LO)
-            col = jnp.where(arrival, slot * n + k * CH, jnp.where(e == 0, B, LO) * n + j * CH)
-            row = jnp.where(arrival, jnp.where(j == 0, A, B), jnp.where(e == 0, A, UP))
-            wanted = jnp.where(
-                arrival,
-                jnp.where(j < 2, has_up, jnp.logical_and(j == 2, jnp.logical_not(lo_down))).astype(jnp.int32),
-                jnp.where(e == 0, second, first).astype(jnp.int32),
-            )
-            pl.when(wanted == 1)(lambda: pair(col, row * n))
-            return 0
-
-        lax.fori_loop(0, chunks, unit, 0)
-        return 0
-
-    lax.fori_loop(0, end + 1, stage, 0)
-
     def finish(slot):
         for t in range(n // 128):
             at = pl.ds(pl.multiple_of(slot * n + t * 128, 128), 128)
@@ -293,20 +242,85 @@
     send_vec_lo = copy(vec.at[LO], got.at[2], vec_send.at[2], vec_recv.at[2], below)
     send_vec_sib = copy(vec.at[1 - core], got.at[0], vec_send.at[0], vec_recv.at[0], sibling)
 
+    def stage(e, _):
+        arrival = e >= 1
+        k = jnp.maximum(e - 1, 0)
+        k = jnp.where(first, k, lax.rem(k, 2) * half + k // 2)
+
+        @pl.when(e == 1)
+        def _():
+            pl.when(has_up)(meta_down.wait_recv)
+            pl.when(has_up)(lambda: spread(UP))
+            pl.when(has_lo)(meta_up.wait_recv)
+            pl.when(has_lo)(lambda: spread(LO))
+
+            @pl.when(second)
+            def _():
+                ups[WAIT_B].wait_send()
+                send_third()
+                for j in range(half):
+                    forward(j)
+
+        @pl.when(jnp.logical_and(first, e == jnp.where(high, 2, STAGE_A)))
+        def _():
+            send_third()
+            for j in range(half):
+                forward(j)
+
+        full = e == chunks
+
+        def unit(j, _):
+            newest = j >= chunks
+
+            @pl.when(jnp.logical_and(jnp.logical_and(arrival, j == 0), has_lo))
+            def _():
+                copy(emb_part(k), rows.at[part(LO, k)], lo_send.at[k], lo_recv.at[k], up).wait_recv()
+
+            @pl.when(jnp.logical_and(jnp.logical_and(arrival, j == chunks), has_up))
+            def _():
+                copy(emb_part(k), rows.at[part(UP, k)], up_send.at[k], up_recv.at[k], down).wait_recv()
+
+            from_lo = jnp.logical_and(arrival, j == 0)
+            slot = jnp.where(arrival, jnp.where(from_lo, LO, UP), B)
+            chunk = jnp.where(arrival, jnp.where(jnp.logical_or(from_lo, newest), k, j - 1), j)
+            row = jnp.where(
+                arrival, jnp.where(from_lo, B, jnp.where(newest, jnp.where(j == chunks + 2, LO, j - chunks), LO)), A
+            )
+            crossing = jnp.logical_and(first, full)
+            wanted = jnp.where(
+                arrival,
+                jnp.where(
+                    from_lo,
+                    jnp.logical_not(lo_down).astype(jnp.int32),
+                    jnp.where(
+                        jnp.logical_and(newest, j < chunks + 2), has_up.astype(jnp.int32), crossing.astype(jnp.int32)
+                    ),
+                ),
+                jnp.logical_and(second, j < chunks).astype(jnp.int32),
+            )
+            pl.when(wanted == 1)(lambda: pair(slot * n + chunk * CH, row * n))
+
+            @pl.when(jnp.logical_and(jnp.logical_and(has_lo, full), j == (chunks + 2) * (1 - core)))
+            def _():
+                finish(LO)
+                send_vec_lo.start()
+
+            return 0
+
+        lax.fori_loop(0, chunks + 3, unit, 0)
+        return 0
+
+    lax.fori_loop(0, chunks + 1, stage, 0)
+
     @pl.when(has_up)
     def _():
         finish(UP)
         send_vec_up.start()
 
-    @pl.when(has_lo)
-    def _():
-        finish(LO)
-        send_vec_lo.start()
-
     finish(1 - core)
     send_vec_sib.start()
     finish(core)
-    best = jnp.maximum(vec[core], -2.0)
+    best = vec[core]
     got_down, got_up = send_down, send_up
     send_vec_sib.wait_recv()
     best = jnp.maximum(best, got[0])
@@ -373,7 +387,7 @@
         ),
         name="neighbour_cosines",
     )(embeddings, cluster_ids.reshape(1, n), valid_counts)
-    return best.reshape(n)
+    return lax.optimization_barrier(jnp.maximum(best, -2.0)).reshape(n)
 
 
 def solution(mesh):

time: 52.5 us -> 51.6 us (0.983); the launches traced: 52.3 us -> 50.7 us
  Pallas kernels: 50.4 us -> 48.8 us
  other arithmetic: 0 us -> 1.28 us
  local copies, waits for them, and re-layouts: 1.28 us -> 0 us
    pallas_call x1, Pallas kernels: 50.4 us -> 48.8 us  [shards(): pl.pallas_call(functools.partial(kernel, blocks), out_shape=jax.ShapeDtyp...]
    max x0 -> x1, other arithmetic: none -> 1.28 us  [shards(): return lax.optimization_barrier(jnp.maximum(best, -2.0)).reshape(n)]
    unnamed x1 -> x0, local copies, waits for them, and re-layouts: 1.28 us -> none
where the time goes in v4:
time: 51.6 us; the launch traced here: 50.7 us
  Pallas kernels  48.8 us (95%)
  other arithmetic  1.28 us (2%)
  between operations  0.66 us (1%)
    pallas_call x1, Pallas kernels, shards(): pl.pallas_call(functools.partial(kernel, blocks), out_shape=jax.ShapeDtyp...  48.8 us
    max x1, other arithmetic, shards(): return lax.optimization_barrier(jnp.maximum(best, -2.0)).reshape(n)  1.28 us

profile of v4, /device:TPU:1, one launch (start us, length us, event | category | flops | bytes accessed | tf_op | source)
XLA Modules:
  0.0 50.7 jit_solution(5317467757738900912)
XLA Ops:
  0.7 48.8 %neighbour_cosines.1 = f32[8,128]{1,0:T(8,128)} custom-call(bf16[1024,768]{1,0:T(8,128)(2,1)} %emb.1, s32[1,1024]{1,0:T(1,128)} %bitcast.2, s32[1]{0:T(128)S(6)} %copy.4.count), custom_call_target="tpu_custom_call" | custom-call | tf_op jit(solution)/shard_map/neighbour_cosines/pallas_call | solution.py:362
  49.4 1.3 %broadcast_maximum_fusion = f32[8,128]{1,0:T(8,128)} fusion(f32[8,128]{1,0:T(8,128)} %neighbour_cosines.1), kind=kLoop, calls=%fused_computation | loop fusion | flops 1024 | bytes 8192 | tf_op jit(solution)/shard_map/max | solution.py:390

commit v5 on v4

--- a/solution.py
+++ b/solution.py
@@ -233,9 +233,9 @@
     def finish(slot):
         for t in range(n // 128):
             at = pl.ds(pl.multiple_of(slot * n + t * 128, 128), 128)
-            best = jnp.maximum(
-                jnp.max(racc[at, :].T, axis=0, keepdims=True), jnp.max(cacc[:, at], axis=0, keepdims=True)
-            )
+            best = jnp.max(cacc[:, at], axis=0, keepdims=True)
+            if not (isinstance(slot, int) and slot == UP):
+                best = jnp.maximum(best, jnp.max(racc[at, :].T, axis=0, keepdims=True))
             vec[slot, t : t + 1, :] = best * cmeta[0:1, at]
 
     send_vec_up = copy(vec.at[UP], got.at[1], vec_send.at[1], vec_recv.at[1], above)
@@ -284,7 +284,7 @@
             slot = jnp.where(arrival, jnp.where(from_lo, LO, UP), B)
             chunk = jnp.where(arrival, jnp.where(jnp.logical_or(from_lo, newest), k, j - 1), j)
             row = jnp.where(
-                arrival, jnp.where(from_lo, B, jnp.where(newest, jnp.where(j == chunks + 2, LO, j - chunks), LO)), A
+                arrival, jnp.where(from_lo, B, jnp.where(j > chunks, j - chunks - 1, LO)), A
             )
             crossing = jnp.logical_and(first, full)
             wanted = jnp.where(
@@ -293,14 +293,14 @@
                     from_lo,
                     jnp.logical_not(lo_down).astype(jnp.int32),
                     jnp.where(
-                        jnp.logical_and(newest, j < chunks + 2), has_up.astype(jnp.int32), crossing.astype(jnp.int32)
+                        j > chunks, has_up.astype(jnp.int32), crossing.astype(jnp.int32)
                     ),
                 ),
                 jnp.logical_and(second, j < chunks).astype(jnp.int32),
             )
             pl.when(wanted == 1)(lambda: pair(slot * n + chunk * CH, row * n))
 
-            @pl.when(jnp.logical_and(jnp.logical_and(has_lo, full), j == (chunks + 2) * (1 - core)))
+            @pl.when(jnp.logical_and(jnp.logical_and(has_lo, full), j == chunks * (1 - core)))
             def _():
                 finish(LO)
                 send_vec_lo.start()
@@ -383,7 +383,7 @@
             dma((3,)), dma((3,)), dma((3,)), dma((3,)),
         ],
         compiler_params=pltpu.CompilerParams(
-            collective_id=0, has_side_effects=True, vmem_limit_bytes=56 * 2**20
+            collective_id=0, has_side_effects=True, vmem_limit_bytes=53 * 2**20
         ),
         name="neighbour_cosines",
     )(embeddings, cluster_ids.reshape(1, n), valid_counts)

time: 51.6 us -> 50.2 us (0.973)
  Pallas kernels: 48.8 us -> 47.6 us
  other arithmetic: 1.28 us -> 0.6 us
  local copies, waits for them, and re-layouts: 0 us -> 0.68 us
    pallas_call x1, Pallas kernels: 48.8 us -> 47.6 us  [shards(): pl.pallas_call(functools.partial(kernel, blocks), out_shape=jax.ShapeDtyp...]
    max x1, other arithmetic: 1.28 us -> 0.6 us  [shards(): return lax.optimization_barrier(jnp.maximum(best, -2.0)).reshape(n)]
    unnamed x0 -> x2, local copies, waits for them, and re-layouts: none -> 0.68 us
where the time goes in v5:
time: 50.2 us; the launch traced here: 49.6 us
  Pallas kernels  47.6 us (95%)
  local copies, waits for them, and re-layouts  0.68 us (1%)
  between operations  0.67 us (1%)
  other arithmetic  0.6 us (1%)
    pallas_call x1, Pallas kernels, shards(): pl.pallas_call(functools.partial(kernel, blocks), out_shape=jax.ShapeDtyp...  47.6 us

profile of v5, /device:TPU:1, one launch (start us, length us, event | category | flops | bytes accessed | tf_op | source)
XLA Modules:
  0.0 49.6 jit_solution(4120367537131931590)
XLA Ops:
  0.7 0.0 copy-start
  0.7 0.7 %copy-done = s32[1024]{0:T(1024)S(1)} copy-done((s32[1024]{0:T(1024)S(1)}, s32[1024]{0:T(1024)}, u32[]{:S(2)}) %copy-start) | copy-done | bytes 4120
  1.3 47.6 %neighbour_cosines.1 = f32[8,128]{1,0:T(8,128)S(1)} custom-call(bf16[1024,768]{1,0:T(8,128)(2,1)} %emb.1, s32[1,1024]{1,0:T(1,128)S(1)} %bitcast.2, s32[1]{0:T(128)S(6)} %copy.4.count), custom_call_target="tpu_custom_call" | custom-call | tf_op jit(solution)/shard_map/neighbour_cosines/pallas_call | solution.py:362
  49.0 0.6 %broadcast_maximum_fusion = f32[8,128]{1,0:T(8,128)} fusion(f32[8,128]{1,0:T(8,128)S(1)} %neighbour_cosines.1), kind=kLoop, calls=%fused_computation | loop fusion | flops 1024 | bytes 8192 | tf_op jit(solution)/shard_map/max | solution.py:390
Async XLA Ops:
  0.7 0.7 %copy-start = (s32[1024]{0:T(1024)S(1)}, s32[1024]{0:T(1024)}, u32[]{:S(2)}) copy-start(s32[1024]{0:T(1024)} %param.4) | copy-start | bytes 12292

commit v6 on v5

--- a/solution.py
+++ b/solution.py
@@ -320,7 +320,7 @@
     finish(1 - core)
     send_vec_sib.start()
     finish(core)
-    best = vec[core]
+    best = jnp.maximum(vec[core], -2.0)
     got_down, got_up = send_down, send_up
     send_vec_sib.wait_recv()
     best = jnp.maximum(best, got[0])
@@ -387,7 +387,7 @@
         ),
         name="neighbour_cosines",
     )(embeddings, cluster_ids.reshape(1, n), valid_counts)
-    return lax.optimization_barrier(jnp.maximum(best, -2.0)).reshape(n)
+    return best.reshape(n)
 
 
 def solution(mesh):

time: 50.2 us -> 50.2 us (level)
  other arithmetic: 0.6 us -> 0 us
  local copies, waits for them, and re-layouts: 0.68 us -> 1.28 us
    max x1 -> x0, other arithmetic: 0.6 us -> none  [shards(): return lax.optimization_barrier(jnp.maximum(best, -2.0)).reshape(n)]
    unnamed x2 -> x3, local copies, waits for them, and re-layouts: 0.68 us -> 1.28 us
where the time goes in v6:
time: 50.2 us; the launch traced here: 49.6 us
  Pallas kernels  47.6 us (95%)
  local copies, waits for them, and re-layouts  1.28 us (3%)
  between operations  0.67 us (1%)
    pallas_call x1, Pallas kernels, shards(): pl.pallas_call(functools.partial(kernel, blocks), out_shape=jax.ShapeDtyp...  47.6 us
    unnamed x3, local copies, waits for them, and re-layouts  1.28 us

profile of v6, /device:TPU:1, one launch (start us, length us, event | category | flops | bytes accessed | tf_op | source)
XLA Modules:
  0.0 49.6 jit_solution(1392980836288951372)
XLA Ops:
  0.7 0.0 copy-start
  0.7 0.7 %copy-done = s32[1024]{0:T(1024)S(1)} copy-done((s32[1024]{0:T(1024)S(1)}, s32[1024]{0:T(1024)}, u32[]{:S(2)}) %copy-start) | copy-done | bytes 4120
  1.3 47.6 %neighbour_cosines.1 = f32[8,128]{1,0:T(8,128)S(1)} custom-call(bf16[1024,768]{1,0:T(8,128)(2,1)} %emb.1, s32[1,1024]{1,0:T(1,128)S(1)} %bitcast.3, s32[1]{0:T(128)S(6)} %copy.5.count), custom_call_target="tpu_custom_call" | custom-call | tf_op jit(solution)/shard_map/neighbour_cosines/pallas_call | solution.py:362
  49.0 0.6 %copy.6 = f32[1024]{0:T(1024)} copy(f32[1024]{0:T(1024)S(1)} %bitcast.2) | data formatting | bytes 8192
Async XLA Ops:
  0.7 0.7 %copy-start = (s32[1024]{0:T(1024)S(1)}, s32[1024]{0:T(1024)}, u32[]{:S(2)}) copy-start(s32[1024]{0:T(1024)} %param.4) | copy-start | bytes 12292
